TPU v7x, 256 devices: a whole 4x4x8 slice. The times are simulated.
256 devices in a mesh: req: 32 (over y, z), head: 8 (over x, core).
Axes of the slice: x: 4, y: 4, z: 8, core: 2. Of those that a mesh axis runs over, the one named last changes fastest.
Arguments:
- kv_pool: bfloat16 [5120, 8, 128, 256], P('req', 'head'), may hold values from -6 to 6
- block_table: int32 [1024, 5], P('req'), may hold values from 0 to 159, as said below
- lengths: int32 [1024], replicated, may hold values from 1 to 640, as said below
- new_slot: int32 [1024], replicated, may hold values from 0 to 1023, as said below
- queries: bfloat16 [1024, 2, 8192], P('req', None, 'head'), may hold values from -200 to 200
- new_kv: bfloat16 [1024, 2, 8, 256], P('req', None, 'head'), may hold values from -8 to 8
- output_weight: bfloat16 [8192, 8192], P('head', 'req'), may hold values from -0.0625 to 0.0625
- residual: bfloat16 [1024, 2, 8192], P('head', None, 'req'), may hold values from -6 to 6
Outputs:
- hidden_out: bfloat16 [1024, 2, 8192], P('head', None, 'req')
Inputs may be any that keep to these rules, and one draw needn't show every extreme that they name: `lengths`: on each of a quarter of the devices some request holds exactly 640 tokens. `new_slot`: A permutation made of swaps: device d trades exactly 2 requests with device (d + 32 / 2) mod 32, or none, half of the devices trading; a request that changes device holds at most 4 pages, and on some devices each of the 2 traded requests holds exactly 4 pages. `block_table`: pages of one device's requests are distinct pages of that device's 160; entries past a request's last page are 0 and unused.
All inputs are finite; a program needn't handle non-finite values.
Results may differ from a plain program's by a relative error of at most 0.0075.
Values may be sent and summed in bfloat16 or wider, within the bound.
A program may use at most 128 MiB of HBM per device.

v0:
```python
import math

import jax
import jax.numpy as jnp
from jax import lax
from jax.sharding import PartitionSpec as P

MOVE_PAGES = 4
SWAP = 2


NEG_FILL = -1e30


def from_partner(block, axis, stride):
    count = lax.axis_size(axis)
    route = []
    for low in range(count):
        high = low | 1 << stride
        if high != low and high < count:
            route += [(low, high), (high, low)]
    return lax.ppermute(block, axis, route)


def cache_partial(cached, lengths_here, query_rows, head_size):
    row_total, kv_here, span, width = cached.shape
    step_count = query_rows.shape[1]
    grouped = query_rows.reshape(row_total, step_count, kv_here, -1, head_size)
    scaling = 1.0 / math.sqrt(head_size)
    scores = (
        jnp.einsum(
            "nskgd,nktd->nskgt",
            grouped,
            cached[..., :head_size],
            preferred_element_type=jnp.float32,
        )
        * scaling
    )
    valid = jnp.arange(span)[None, :] < lengths_here[:, None]
    scores = jnp.where(valid[:, None, None, None, :], scores, NEG_FILL)
    top = jnp.max(scores, -1)
    weights = jnp.exp(scores - top[..., None])
    total = jnp.sum(weights, -1)
    mixed = jnp.einsum(
        "nskgt,nktd->nskgd",
        weights.astype(jnp.bfloat16),
        cached[..., head_size:],
        preferred_element_type=jnp.float32,
    )
    return (top, total, mixed)


def fresh_partial(query_rows, new_kv, head_size):
    row_total, step_count, kv_here, width = new_kv.shape
    grouped = query_rows.reshape(row_total, step_count, kv_here, -1, head_size)
    scaling = 1.0 / math.sqrt(head_size)
    scores = (
        jnp.einsum(
            "nskgd,nukd->nskgu",
            grouped,
            new_kv[..., :head_size],
            preferred_element_type=jnp.float32,
        )
        * scaling
    )
    causal = jnp.arange(step_count)[None, :] <= jnp.arange(step_count)[:, None]
    scores = jnp.where(causal[None, :, None, None, :], scores, NEG_FILL)
    top = jnp.max(scores, -1)
    weights = jnp.exp(scores - top[..., None])
    total = jnp.sum(weights, -1)
    mixed = jnp.einsum(
        "nskgu,nukd->nskgd",
        weights.astype(jnp.bfloat16),
        new_kv[..., head_size:],
        preferred_element_type=jnp.float32,
    )
    return (top, total, mixed)


def merge_parts(first_part, second_part):
    top = jnp.maximum(first_part[0], second_part[0])
    first_factor = jnp.exp(first_part[0] - top)
    second_factor = jnp.exp(second_part[0] - top)
    total = first_part[1] * first_factor + second_part[1] * second_factor
    mixed = first_part[2] * first_factor[..., None] + second_part[2] * second_factor[..., None]
    return mixed / total[..., None]


def per_device(kv_pool, block_table, lengths, new_slot, queries, new_kv, output_weight, residual):
    pair_bit = lax.axis_size("req").bit_length() - 2
    position = lax.axis_index("req")
    slots_here = block_table.shape[0]
    pages_most = block_table.shape[1]
    pool_pages, kv_here, page_size, width = kv_pool.shape
    head_size = width // 2
    slot_total = new_slot.shape[0]
    first_slot = position * slots_here
    local = jnp.arange(slots_here, dtype=jnp.int32)
    target = lax.dynamic_slice_in_dim(new_slot, first_slot, slots_here, 0)
    inverse = jnp.argsort(new_slot)
    reference_device = lax.dynamic_slice_in_dim(inverse, first_slot, slots_here, 0)
    leaving = target // slots_here != position
    arriving = reference_device // slots_here != position
    leave_order = jnp.argsort(jnp.where(leaving, target, slot_total + local))
    arrive_rank = jnp.cumsum(arriving.astype(jnp.int32)) - 1
    leave_slots = leave_order[:SWAP]
    departing_flag = jnp.any(leaving)
    arrive_lengths = lengths[reference_device]
    resident = jnp.transpose(kv_pool[block_table], (0, 2, 1, 3, 4)).reshape(
        slots_here, kv_here, pages_most * page_size, width
    )
    migrating_requests = kv_pool[block_table[leave_slots, :MOVE_PAGES]]
    migrating_requests = jnp.where(
        departing_flag, migrating_requests, jnp.zeros_like(migrating_requests)
    )
    received = from_partner(migrating_requests, "req", pair_bit)
    received = jnp.transpose(received, (0, 2, 1, 3, 4)).reshape(
        SWAP, kv_here, MOVE_PAGES * page_size, width
    )
    received = jnp.pad(
        received, ((0, 0), (0, 0), (0, (pages_most - MOVE_PAGES) * page_size), (0, 0))
    )
    stacked = jnp.concatenate([resident, received], 0)
    pick_rows = jnp.where(arriving, slots_here + arrive_rank, reference_device - first_slot)
    cached = stacked[pick_rows]
    cache_part = cache_partial(cached, arrive_lengths, queries, head_size)
    fresh = fresh_partial(queries, new_kv, head_size)
    attended = (
        merge_parts(cache_part, fresh)
        .reshape(slots_here, queries.shape[1], -1)
        .astype(jnp.bfloat16)
    )
    collected_rows = lax.all_gather(attended, "req", axis=0, tiled=True)
    summed = lax.psum_scatter(
        jnp.einsum(
            "flg,gz->flz", collected_rows, output_weight, preferred_element_type=jnp.float32
        ).astype(jnp.bfloat16),
        "head",
        scatter_dimension=0,
        tiled=True,
    ).astype(jnp.float32)
    return (residual.astype(jnp.float32) + summed).astype(jnp.bfloat16)


def solution(mesh):
    in_specs = (
        P("req", "head", None, None),
        P("req", None),
        P(),
        P(),
        P("req", None, "head"),
        P("req", None, "head", None),
        P("head", "req"),
        P("head", None, "req"),
    )
    out_specs = P("head", None, "req")
    return jax.shard_map(
        per_device, mesh=mesh, in_specs=in_specs, out_specs=out_specs, check_vma=False
    )
```

profile of v0, /device:TPU:9, one launch (start us, length us, event | category | flops | bytes accessed | tf_op | source)
XLA Modules:
  0.0 199.7 jit_solution(15560846240896983928)
XLA Ops:
  6.5 5.1 %sort.35 = (s32[1024]{0:T(1024)}, s32[1024]{0:T(1024)S(1)}) sort(s32[1024]{0:T(1024)} %param.11, s32[1024]{0:T(1024)S(1)} %iota.35), dimensions={0}, to_apply=%region_2.3 | sort | flops 10240 | bytes 16384 | tf_op jit(solution)/shard_map/jit(argsort)/sort | solution.py:100
  11.7 1.4 compare_reduce_fusion
  13.3 0.1 add_reduce_fusion
  13.4 0.8 compare_select_fusion.4
  14.2 1.7 sort.34
  15.9 0.7 iota_add_fusion.2
  16.6 1.3 gather_fusion.7
  18.0 1.3 gather_fusion.6
  19.3 1.3 gather_fusion.4
  20.6 1.3 gather_fusion.5
  21.9 0.1 copy.39
  22.1 4.6 %gather_fusion.1 = bf16[8,128,256]{2,1,0:T(8,128)(2,1)S(1)} fusion(bf16[160,128,256]{2,1,0:T(8,128)(2,1)} %bitcast.126, s32[1024]{0:T(1024)S(1)} %pad_clamp_fusion.2), kind=kCustom, calls=%fused_computation.1 | custom fusion | bytes 1048608 | tf_op jit(solution)/shard_map/gather | solution.py:112
  26.7 0.7 broadcast_select_fusion
  27.4 2.1 %collective-permute-start = (bf16[2,4,1,128,256]{4,3,1,0,2:T(8,128)(2,1)S(1)}, bf16[2,4,1,128,256]{4,3,1,0,2:T(8,128)(2,1)S(1)}, u32[]{:S(2)}, u32[]{:S(2)}) collective-permute-start(bf16[2,4,1,128,256]{4,3,1,0,2:T(8,128)(2,1)S(1)} %bitcast.131), channel_id=1, source_target_pairs={{0,128},{128,0},{8,136},{136,8},{16,144},{144,16},{24,152},{152,24... | collective-permute-start | bytes 1572872 | tf_op jit(solution)/shard_map/ppermute | solution.py:22
  29.5 0.7 compare_select_fusion
  30.3 0.1 reshape.194
  30.4 11.3 %gather_fusion = bf16[160,128,256]{2,1,0:T(8,128)(2,1)} fusion(bf16[160,128,256]{2,1,0:T(8,128)(2,1)} %bitcast.127, s32[1024]{0:T(1024)S(1)} %pad_clamp_fusion.3), kind=kCustom, calls=%fused_computation | custom fusion | bytes 20972160 | tf_op jit(solution)/shard_map/gather | solution.py:109
  41.8 0.7 fusion.35
  42.6 0.1 fusion.24
  42.9 0.7 gather_fusion.3
  43.6 10.2 %fusion.2 = bf16[34,640,256]{2,1,0:T(8,128)(2,1)} fusion(bf16[2,1,512,256]{3,2,0,1:T(8,128)(2,1)S(1)} %bitcast.130, bf16[32,1,640,256]{3,2,0,1:T(8,128)(2,1)} %bitcast.125), kind=kLoop, calls=%fused_computation.11 | loop fusion | flops 33423360 | bytes 22151168 | tf_op jit(solution)/shard_map/concatenate | solution.py:123
  53.9 10.0 %gather_fusion.2 = bf16[32,640,256]{2,1,0:T(8,128)(2,1)} fusion(bf16[34,640,256]{2,1,0:T(8,128)(2,1)} %fusion.2, s32[1024]{0:T(1024)S(1)} %pad_clamp_fusion.1), kind=kCustom, calls=%fused_computation.2 | custom fusion | bytes 20971648 | tf_op jit(solution)/shard_map/gather | solution.py:125
  63.9 4.3 %bitcast_reduce_fusion = (f32[32,2,8]{2,1,0:T(2,128)S(1)}, f32[32,1,640,2,8]{2,4,3,0,1:T(8,128)S(1)}) fusion(bf16[32,2,8,128]{3,2,1,0:T(8,128)(2,1)S(1)} %reshape.184, bf16[32,1,640,256]{3,2,0,1:T(8,128)(2,1)} %bitcast.128, pred[32,640]{1,0:T(8,128)(4,1)S(1)} %iota_compare_fusion.1), kind=kOutput, calls=%fused_computation.20 | convolution fusion | flops 84868608 | bytes 6707200 | tf_op jit(solution)/shard_map/nskgd,nktd->nskgt/dot_general | solution.py:31
  68.3 0.4 fusion.14
  68.9 3.5 %fusion.13 = f32[32,1,128,2,8]{2,4,3,0,1:T(8,128)S(1)} fusion(bf16[32,1,640,256]{3,2,0,1:T(8,128)(2,1)} %bitcast.129, f32[32,1,640,2,8]{2,4,3,0,1:T(8,128)S(1)} %get-tuple-element.23, f32[32,2,8]{2,1,0:T(2,128)S(1)} %get-tuple-element.22, f32[32,2,8]{2,1,0:T(2,128)S(1)} %copy.45), kind=kOutput, calls=%fused_computation.28 | convolution fusion | flops 84606976 | bytes 6819840 | tf_op jit(solution)/shard_map/nskgt,nktd->nskgd/dot_general | solution.py:44
  72.6 0.3 fusion.17
  73.0 0.7 copy.52
  73.8 79.9 %all-gather.2.cloned.1.call-done = bf16[1024,2,1024]{2,0,1:T(8,128)(2,1)} async-done(((bf16[32,2,1024]{2,0,1:T(8,128)(2,1)}), bf16[1024,2,1024]{2,0,1:T(8,128)(2,1)}) %all-gather.2.cloned.1.call-update) | async-done | bytes 4194320 | tf_op jit(solution)/shard_map/all_gather | solution.py:133
  153.6 4.4 %convolution_convert_fusion = bf16[1024,2,256]{2,0,1:T(8,128)(2,1)} fusion(bf16[1024,2,1024]{2,0,1:T(8,128)(2,1)} %all-gather.2.cloned.1.call-done, bf16[1024,256]{1,0:T(8,128)(2,1)S(1)} %copy-done), kind=kOutput, calls=%fused_computation.16 | convolution fusion | flops 1074266112 | bytes 5767168 | tf_op jit(solution)/shard_map/flg,gz->flz/dot_general | solution.py:135
  158.1 33.1 %reduce-scatter.2.cloned.1.call-done = bf16[128,2,256]{2,0,1:T(8,128)(2,1)} async-done(((bf16[1024,2,256]{2,0,1:T(8,128)(2,1)}), bf16[128,2,256]{2,0,1:T(8,128)(2,1)}) %reduce-scatter.2.cloned.1.call-update) | async-done | bytes 131088 | tf_op jit(solution)/shard_map/reduce_scatter | solution.py:134
  191.1 0.9 add_convert_fusion
  192.1 0.8 copy.53
  (46 shorter events, 1.4 us)
Async XLA Ops:
  6.5 147.1 %copy-start = (bf16[1024,256]{1,0:T(8,128)(2,1)S(1)}, bf16[1024,256]{1,0:T(8,128)(2,1)}, u32[]{:S(2)}) copy-start(bf16[1024,256]{1,0:T(8,128)(2,1)} %param.14) | copy-start | bytes 1572868
  6.5 147.1 %all-gather.2.cloned.1.call-start = ((), (), s32[]{:S(2)}) async-start(), calls=%async_computation.1 | async-start | bytes 4325376 | tf_op jit(solution)/shard_map/all_gather | solution.py:133
  27.4 16.2 %collective-permute-start = (bf16[2,4,1,128,256]{4,3,1,0,2:T(8,128)(2,1)S(1)}, bf16[2,4,1,128,256]{4,3,1,0,2:T(8,128)(2,1)S(1)}, u32[]{:S(2)}, u32[]{:S(2)}) collective-permute-start(bf16[2,4,1,128,256]{4,3,1,0,2:T(8,128)(2,1)S(1)} %bitcast.131), channel_id=1, source_target_pairs={{0,128},{128,0},{8,136},{136,8},{16,144},{144,16},{24,152},{152,24... | collective-permute-start | bytes 1572872 | tf_op jit(solution)/shard_map/ppermute | solution.py:22
  30.4 11.3 %copy-start.3 = (bf16[32,2,1024]{2,1,0:T(2,128)(2,1)S(1)}, bf16[32,2,1024]{2,1,0:T(2,128)(2,1)}, u32[]{:S(2)}) copy-start(bf16[32,2,1024]{2,1,0:T(2,128)(2,1)} %param.12) | copy-start | bytes 393220
  30.4 11.4 %copy-start.4 = (bf16[32,2,1,256]{3,1,2,0:T(2,128)(2,1)S(1)}, bf16[32,2,1,256]{3,1,2,0:T(2,128)(2,1)}, u32[]{:S(2)}) copy-start(bf16[32,2,1,256]{3,1,2,0:T(2,128)(2,1)} %param.13) | copy-start | bytes 98308
  30.4 12.4 %copy-start.1 = (s32[1024]{0:T(1024)S(1)}, s32[1024]{0:T(1024)}, u32[]{:S(2)}) copy-start(s32[1024]{0:T(1024)} %param.10) | copy-start | bytes 12292
  68.9 122.2 %copy-start.2 = (bf16[128,2,256]{2,1,0:T(2,128)(2,1)S(1)}, bf16[128,2,256]{2,1,0:T(2,128)(2,1)}, u32[]{:S(2)}) copy-start(bf16[128,2,256]{2,1,0:T(2,128)(2,1)} %param.15) | copy-start | bytes 393220
  73.7 117.4 %reduce-scatter.2.cloned.1.call-start = ((), (), s32[]{:S(2)}) async-start(), calls=%async_computation.2 | async-start | bytes 1179648 | tf_op jit(solution)/shard_map/reduce_scatter | solution.py:134
Sparse Core Ops, SparseCore 0:
  73.8 79.7 all-gather.1
  158.2 32.8 reduce-scatter.1
where the time goes:
time: 203 us; the launch traced here: 200 us
  waiting for transfers between devices  113 us (56%)
  local copies, waits for them, and re-layouts  34.5 us (17%)
  other arithmetic  23.2 us (11%)
  between operations  13.6 us (7%)
  matrix products  13.3 us (7%)
  starting transfers between devices  2.15 us (1%)
    all_gather x1, waiting for transfers between devices, per_device(): collected_rows = lax.all_gather(attended, 'req', axis=0, tiled=True)  79.9 us
    reduce_scatter x1, waiting for transfers between devices, per_device(): lax.psum_scatter(jnp.einsum('flg,gz->flz', collected_rows, output_weight,...  33.1 us
    gather x1, local copies, waits for them, and re-layouts, per_device(): kv_pool[block_table]  11.3 us
    concatenate x1, other arithmetic, per_device(): stacked = jnp.concatenate([resident, received], 0)  10.2 us
    gather x1, local copies, waits for them, and re-layouts, per_device(): cached = stacked[pick_rows]  10 us
    gather x6, local copies, waits for them, and re-layouts, per_device(): migrating_requests = kv_pool[block_table[leave_slots, :MOVE_PAGES]]  9.94 us
    sort x1, other arithmetic, per_device(): inverse = jnp.argsort(new_slot)  5.11 us
    dot_general x1, matrix products, per_device(): jnp.einsum('flg,gz->flz', collected_rows, output_weight, preferred_elemen...  4.42 us
  transfers between devices with their start and end apart: 3, of which 2 were waited for; matrix products, arithmetic and copies ran while one was open for 7% of the time, Pallas kernels for 0%

commit v1 on v0

v1 whole, which is shorter than its diff:
```python
import functools
import math

import jax
import jax.numpy as jnp
from jax import lax
from jax.experimental import pallas as pl
from jax.experimental.pallas import tpu as pltpu
from jax.sharding import PartitionSpec as P

MESH = pl.DeviceIdType.MESH
NEG_FILL = -1e30
NT = (((1,), (1,)), ((), ()))
NN = (((1,), (0,)), ((), ()))


def dot(a, b, dims=NN):
    return lax.dot_general(a, b, dims, preferred_element_type=jnp.float32)


def scan_leaving(new_slot, device):
    def body(e, carry):
        count, i0, i1, t0, t1 = carry
        v = new_slot[device * 32 + e]
        leaves = jnp.where((v >> 5) != device, 1, 0)
        first = (leaves == 1) & (count == 0)
        second = (leaves == 1) & (count == 1)
        return (
            count + leaves,
            jnp.where(first, e, i0),
            jnp.where(second, e, i1),
            jnp.where(first, v & 31, t0),
            jnp.where(second, v & 31, t1),
        )

    zero = jnp.int32(0)
    return lax.fori_loop(
        0, 32, body, (zero, zero, zero, jnp.int32(30), jnp.int32(31)), unroll=4
    )


def kernel(
    pool, weight, queries, fresh2, fresh3, residual, table, lengths, new_slot, out,
    pool_v, w_v, q_v, f2_v, f3_v, res_v, fv_v, att_v, attended, qx_s, qx_r, ret_s, ret_r,
    c_s, c_r, own_v, y_s, y_r, x_r, perm_v,
    l_sem, qx_sem, ret_sem, w_ss, w_rs, z_ss, z_rs, c_ss, c_rs, y_ss, y_rs, x_ss, x_rs,
):
    req, head = lax.axis_index("req"), lax.axis_index("head")
    x, core = head // 2, head % 2
    y, z = req // 8, req % 8
    partner = (req + 16) % 32

    def at(dx=0, dy=0, dz=0, flip=0):
        return (
            ((y + dy) % 4) * 8 + (z + dz) % 8,
            ((x + dx) % 4) * 2 + (core + flip) % 2,
        )

    def remote(src, dst, ss, rs, device):
        return pltpu.make_async_remote_copy(
            src_ref=src, dst_ref=dst, send_sem=ss, recv_sem=rs,
            device_id=device, device_id_type=MESH,
        )

    barrier = pltpu.get_barrier_semaphore()
    peers = [at(dz=d) for d in (1, 7, 2, 6)]
    peers += [at(dy=d) for d in (1, 3, 2)]
    peers += [at(dx=d) for d in (1, 3, 2)]
    peers += [at(flip=1)]
    for peer in peers:
        pl.semaphore_signal(barrier, inc=1, device_id=peer, device_id_type=MESH)

    load_q = pltpu.make_async_copy(queries, q_v, l_sem.at[0])
    load_f2 = pltpu.make_async_copy(fresh2, f2_v, l_sem.at[1])
    load_f3 = pltpu.make_async_copy(fresh3, f3_v, l_sem.at[2])
    load_w = pltpu.make_async_copy(weight, w_v.at[0], l_sem.at[3])
    load_pool = pltpu.make_async_copy(pool, pool_v, l_sem.at[4])
    load_res = pltpu.make_async_copy(residual, res_v, l_sem.at[5])
    for load in (load_q, load_f2, load_f3, load_w, load_pool, load_res):
        load.start()

    _, i0, i1, _, _ = scan_leaving(new_slot, req)
    trades, _, _, t0, t1 = scan_leaving(new_slot, partner)
    low, high = jnp.minimum(t0, t1), jnp.maximum(t0, t1)

    load_q.wait()
    load_f2.wait()
    load_f3.wait()
    for k, t in enumerate((t0, t1)):
        new_rows = f3_v[t].astype(jnp.float32)
        qx_s[k, 0:16] = q_v[t]
        qx_s[k, 16:32] = jnp.concatenate(
            [new_rows, jnp.zeros((12, 128), jnp.float32)], 0
        ).astype(jnp.bfloat16)
        qx_s[k, 32:48] = jnp.concatenate(
            [new_rows[2:4], jnp.zeros((14, 128), jnp.float32)], 0
        ).astype(jnp.bfloat16)
    fv_v[...] = pltpu.roll(f2_v[...].astype(jnp.float32), 126, 0).astype(jnp.bfloat16)

    pl.semaphore_wait(barrier, len(peers))

    send_q = remote(qx_s, qx_r, qx_sem.at[0], qx_sem.at[1], at(dy=2))
    send_q.start()
    load_w.wait()

    def w_half(d, half):
        return w_v.at[d, pl.ds(half * 512, 512)]

    w_plan = [(0, 3, 1, 0), (1, 1, 3, 1), (1, 3, 1, 2), (0, 1, 3, 3)]
    w_own = [
        remote(w_half(0, half), w_half(d, half), w_ss.at[k], w_rs.at[k], at(dy=dy))
        for half, d, dy, k in w_plan
    ]
    w_own[0].start()
    w_own[1].start()

    t_row = lax.broadcasted_iota(jnp.int32, (128, 256), 0)
    u_col = lax.broadcasted_iota(jnp.int32, (128, 256), 1) & 63
    slot_t = t_row >> 2
    for q in range(4):
        source = x * 8 + core * 4 + q
        _, _, _, a, b = scan_leaving(new_slot, (source + 16) % 32)
        lo, hi = jnp.minimum(a, b), jnp.maximum(a, b)
        last = jnp.where(hi == 30, lo, hi)
        pos = jnp.where(slot_t == 30, lo, slot_t)
        pos = jnp.where(slot_t == 31, last, pos)
        pos = jnp.where(slot_t == lo, 30, pos)
        pos = jnp.where(slot_t == hi, 31, pos)
        row = ((pos >> 3) << 4) + ((t_row & 1) << 3) + (pos & 7)
        for ct in range(2):
            hit = (row == u_col) & (((t_row >> 1) & 1) == ct)
            perm_v[q, ct] = jnp.where(hit, 1.0, 0.0).astype(jnp.bfloat16)

    load_pool.wait()

    scaling = 1.0 / math.sqrt(128)
    lane = lax.broadcasted_iota(jnp.int32, (16, 128), 1)
    odd = (lax.broadcasted_iota(jnp.int32, (16, 128), 0) & 1) == 1

    def attend(query, old, keys_new, values_new, place):
        span = lengths[req * 32 + old]
        pages = [table[p, old] for p in range(5)]
        scores = []
        for p in range(5):
            s = dot(query, pool_v[pages[p], :, 0:128], NT) * scaling
            scores.append(jnp.where(lane < span - 128 * p, s, NEG_FILL))
        s = dot(query, keys_new, NT) * scaling
        seen = (lane == place) | ((lane == place + 1) & odd)
        scores.append(jnp.where(seen, s, NEG_FILL))
        top = functools.reduce(jnp.maximum, scores)
        top = jnp.max(top, axis=1, keepdims=True)
        weights = [jnp.exp(s - top) for s in scores]
        total = jnp.sum(functools.reduce(jnp.add, weights), axis=1, keepdims=True)
        mixed = dot(weights[5].astype(jnp.bfloat16), values_new)
        for p in range(5):
            mixed += dot(weights[p].astype(jnp.bfloat16), pool_v[pages[p], :, 128:256])
        return mixed / total

    def slot_at(p):
        slot = jnp.where(p == low, jnp.where(high == 30, 31, 30), p)
        slot = jnp.where(p == high, 31, slot)
        slot = jnp.where(p == 30, low, slot)
        return jnp.where(p == 31, high, slot)

    def group(c):
        for k in range(8):
            slot = slot_at(jnp.int32(c * 8 + k))
            v = new_slot[req * 32 + slot]
            old = jnp.where((v >> 5) == req, v & 31, slot)
            att_v[k * 16 : k * 16 + 16] = attend(
                q_v[slot], old, f2_v[...], fv_v[...], slot * 4
            )

    def chunk(c):
        return attended.at[z, pl.ds(c * 16, 16)]

    def block(dz, c):
        return attended.at[(z + dz) % 8, pl.ds(c * 16, 16)]

    def publish(c):
        for g in range(8):
            rows = [att_v[pl.ds(2 * g + s, 8, stride=16)] for s in range(2)]
            attended[z, c * 16 : c * 16 + 16, g * 128 : g * 128 + 128] = (
                jnp.concatenate(rows, 0).astype(jnp.bfloat16)
            )
        sends = [
            remote(chunk(c), chunk(c), z_ss.at[c, k], z_rs.at[c, k], at(dz=dz))
            for k, dz in enumerate((1, 7, 2, 6))
        ]
        for k in (2, 3, 0, 1):
            sends[k].start()
        return sends

    def arrive(dz, c, k):
        remote(block(dz, c), block(dz, c), z_ss.at[c, k], z_rs.at[c, k], at(dz=1)).wait_recv()

    def forward(c):
        sends = []
        arrive(6, c, 2)
        sends.append(remote(block(6, c), block(6, c), z_ss.at[c, 4], z_rs.at[c, 4], at(dz=1)))
        if c % 2 == 0:
            sends.append(
                remote(block(6, c), block(6, c), z_ss.at[c, 6], z_rs.at[c, 6], at(dz=2))
            )
        for send in sends:
            send.start()
        arrive(2, c, 3)
        more = [remote(block(2, c), block(2, c), z_ss.at[c, 5], z_rs.at[c, 5], at(dz=7))]
        if c % 2 == 1:
            more.append(
                remote(block(2, c), block(2, c), z_ss.at[c, 6], z_rs.at[c, 6], at(dz=6))
            )
        for send in more:
            send.start()
        return sends + more

    z_sends = []
    group(0)
    z_sends += publish(0)

    send_q.wait_recv()
    pad = jnp.zeros((112, 128), jnp.bfloat16)
    for k, old in enumerate((i0, i1)):
        result = attend(
            qx_r[k, 0:16], old,
            jnp.concatenate([qx_r[k, 16:32], pad], 0),
            jnp.concatenate([qx_r[k, 32:48], pad], 0),
            0,
        )
        ret_s[k] = result.astype(jnp.bfloat16)
    send_ret = remote(ret_s, ret_r, ret_sem.at[0], ret_sem.at[1], at(dy=2))
    send_ret.start()
    w_own[2].start()
    w_own[3].start()

    group(1)
    z_sends += publish(1)
    group(2)
    z_sends += publish(2)
    group(3)
    z_sends += forward(0)
    send_ret.wait_recv()
    for p, t in ((6, low), (7, high)):
        came = ret_r[jnp.where(t == t0, 0, 1)].astype(jnp.float32)
        att_v[p * 16 : p * 16 + 16] = jnp.where(
            trades > 0, came, att_v[p * 16 : p * 16 + 16]
        )
    z_sends += publish(3)

    w_fwd = []
    for half, d, dy, k, came in ((0, 3, 1, 4, 0), (1, 1, 3, 5, 1)):
        w_own[came].wait_recv()
        w_fwd.append(
            remote(w_half(d, half), w_half(2, half), w_ss.at[k], w_rs.at[k], at(dy=dy))
        )
        w_fwd[-1].start()
    for c in (1, 2, 3):
        z_sends += forward(c)
    for c in range(4):
        arrive(7, c, 0)
        arrive(1, c, 1)
        arrive(5, c, 4)
        arrive(3, c, 5)
        arrive(4, c, 6)

    def rows_of(which):
        return attended[pl.ds(which * 4, 4)].reshape(256, 1024)

    def core_copy(d):
        return remote(c_s.at[d], c_r.at[d], c_ss.at[d], c_rs.at[d], at(flip=1))

    def y_copy(d):
        return remote(y_s.at[d], y_r.at[d], y_ss.at[d], y_rs.at[d], at(dy=d))

    def product(which, d):
        return dot(rows_of(which), w_v[d])

    def away(d):
        c_s[d] = product(1 - core, d).astype(jnp.bfloat16)
        core_copy(d).start()

    def near(d):
        own_v[d] = product(core, d)

    def join(d):
        core_copy(d).wait_recv()
        both = own_v[d] + c_r[d].astype(jnp.float32)
        both = both.astype(jnp.bfloat16).reshape(4, 64, 256)
        if d == 0:
            y_r[0] = both
        else:
            y_s[d] = both
            y_copy(d).start()

    def x_move(d):
        i = (y + 4 - d) % 4
        far = remote(y_r.at[d], x_r.at[:, x], x_ss.at[d], x_rs.at[x], (req, i * 2 + core))
        here = pltpu.make_async_copy(y_r.at[d], x_r.at[:, x], x_ss.at[d])
        return i != x, far, here

    def x_start(d):
        other, far, here = x_move(d)

        @pl.when(other)
        def _():
            far.start()

        @pl.when(jnp.logical_not(other))
        def _():
            here.start()

    w_own[2].wait_recv()
    w_own[3].wait_recv()
    for d in (1, 3, 0):
        away(d)
    for d in (1, 3, 0):
        near(d)
    for d in (1, 3):
        join(d)
    for k in (4, 5):
        w_fwd[k - 4].wait_recv()
    away(2)
    near(2)
    join(0)
    x_start(0)
    join(2)
    for d in (1, 3, 2):
        y_copy(d).wait_recv()
        x_start(d)

    for d in range(4):
        other, far, here = x_move(d)

        @pl.when(other)
        def _():
            far.wait_send()

        @pl.when(jnp.logical_not(other))
        def _():
            here.wait()

    for k in range(4):

        @pl.when(k != x)
        def _():
            remote(
                y_r.at[0], x_r.at[:, k], x_ss.at[0], x_rs.at[k], at(dx=1)
            ).wait_recv()

    load_res.wait()
    for q in range(4):
        parts = x_r[q].reshape(256, 256)
        total = dot(perm_v[q, 0], parts[:, 0:128]) + dot(perm_v[q, 1], parts[:, 128:256])
        total += res_v[q * 128 : q * 128 + 128].astype(jnp.float32)
        out[q * 128 : q * 128 + 128] = total.astype(jnp.bfloat16)

    send_q.wait_send()
    send_ret.wait_send()
    for send in w_own + w_fwd + z_sends:
        send.wait_send()
    for d in range(4):
        core_copy(d).wait_send()
    for d in (1, 2, 3):
        y_copy(d).wait_send()


def per_device(kv_pool, block_table, lengths, new_slot, queries, new_kv, output_weight, residual):
    q = queries.reshape(32, 2, 8, 128).transpose(0, 2, 1, 3).reshape(32, 16, 128)
    fresh = new_kv.reshape(32, 2, 2, 128).transpose(0, 2, 1, 3)
    res = residual.reshape(128, 2, 2, 128).transpose(0, 2, 1, 3).reshape(512, 128)
    hbm = pl.BlockSpec(memory_space=pl.ANY)
    smem = pl.BlockSpec(memory_space=pltpu.SMEM)
    vmem = pl.BlockSpec(memory_space=pltpu.VMEM)
    bf16, f32 = jnp.bfloat16, jnp.float32
    sem = pltpu.SemaphoreType.DMA
    out = pl.pallas_call(
        kernel,
        name="decode",
        out_shape=jax.ShapeDtypeStruct((512, 128), bf16),
        in_specs=[hbm] * 6 + [smem] * 3,
        out_specs=vmem,
        scratch_shapes=[
            pltpu.VMEM((160, 128, 256), bf16),
            pltpu.VMEM((4, 1024, 256), bf16),
            pltpu.VMEM((32, 16, 128), bf16),
            pltpu.VMEM((128, 128), bf16),
            pltpu.VMEM((32, 4, 128), bf16),
            pltpu.VMEM((512, 128), bf16),
            pltpu.VMEM((128, 128), bf16),
            pltpu.VMEM((128, 128), f32),
            pltpu.VMEM((8, 64, 1024), bf16),
            pltpu.VMEM((2, 48, 128), bf16),
            pltpu.VMEM((2, 48, 128), bf16),
            pltpu.VMEM((2, 16, 128), bf16),
            pltpu.VMEM((2, 16, 128), bf16),
            pltpu.VMEM((4, 256, 256), bf16),
            pltpu.VMEM((4, 256, 256), bf16),
            pltpu.VMEM((4, 256, 256), f32),
            pltpu.VMEM((4, 4, 64, 256), bf16),
            pltpu.VMEM((4, 4, 64, 256), bf16),
            pltpu.VMEM((4, 4, 64, 256), bf16),
            pltpu.VMEM((4, 2, 128, 256), bf16),
            sem((6,)),
            sem((2,)),
            sem((2,)),
            sem((6,)),
            sem((6,)),
            sem((4, 7)),
            sem((4, 7)),
            sem((4,)),
            sem((4,)),
            sem((4,)),
            sem((4,)),
            sem((4,)),
            sem((4,)),
        ],
        compiler_params=pltpu.CompilerParams(
            collective_id=0, has_side_effects=True, vmem_limit_bytes=48 << 20
        ),
    )(
        kv_pool.reshape(160, 128, 256), output_weight, q, fresh.reshape(128, 128),
        fresh.reshape(32, 4, 128), res, block_table.T, lengths, new_slot,
    )
    return out.reshape(128, 2, 2, 128).transpose(0, 2, 1, 3).reshape(128, 2, 256)


def solution(mesh):
    in_specs = (
        P("req", "head", None, None),
        P("req", None),
        P(),
        P(),
        P("req", None, "head"),
        P("req", None, "head", None),
        P("head", "req"),
        P("head", None, "req"),
    )
    return jax.shard_map(
        per_device, mesh=mesh, in_specs=in_specs,
        out_specs=P("head", None, "req"), check_vma=False,
    )
```

time: 203 us -> 58.4 us (0.29)
  the two profiles are of different devices: /device:TPU:9 before, /device:TPU:4 now
where the time goes in v1:
time: 58.4 us; the launch traced here: 58.1 us
  Pallas kernels  51.8 us (89%)
  local copies, waits for them, and re-layouts  6.32 us (11%)
    pallas_call x1, Pallas kernels, per_device(): pl.pallas_call(kernel, name='decode', out_shape=jax.ShapeDtypeStruct((512...  51.8 us
    unnamed x15, local copies, waits for them, and re-layouts  6.32 us

profile of v1, /device:TPU:4, one launch (start us, length us, event | category | flops | bytes accessed | tf_op | source)
XLA Modules:
  0.0 58.1 jit_solution(6524735787143805301)
XLA Ops:
  0.0 0.0 copy-start
  0.0 1.0 %copy-done = bf16[1024,256]{1,0:T(8,128)(2,1)S(1)} copy-done((bf16[1024,256]{1,0:T(8,128)(2,1)S(1)}, bf16[1024,256]{1,0:T(8,128)(2,1)}, u32[]{:S(2)}) %copy-start) | copy-done | bytes 524312
  1.0 0.0 copy-start.1
  1.0 0.9 %copy-done.1 = bf16[32,2,1024]{2,1,0:T(2,128)(2,1)S(1)} copy-done((bf16[32,2,1024]{2,1,0:T(2,128)(2,1)S(1)}, bf16[32,2,1024]{2,1,0:T(2,128)(2,1)}, u32[]{:S(2)}) %copy-start.1) | copy-done | bytes 131096
  1.9 0.0 copy-start.2
  1.9 0.9 %copy-done.2 = bf16[128,2,256]{2,1,0:T(2,128)(2,1)S(1)} copy-done((bf16[128,2,256]{2,1,0:T(2,128)(2,1)S(1)}, bf16[128,2,256]{2,1,0:T(2,128)(2,1)}, u32[]{:S(2)}) %copy-start.2) | copy-done | bytes 131096
  2.9 0.0 copy-start.3
  2.9 0.8 %copy-done.3 = bf16[32,2,1,256]{3,1,2,0:T(2,128)(2,1)S(1)} copy-done((bf16[32,2,1,256]{3,1,2,0:T(2,128)(2,1)S(1)}, bf16[32,2,1,256]{3,1,2,0:T(2,128)(2,1)}, u32[]{:S(2)}) %copy-start.3) | copy-done | bytes 32792
  3.6 0.0 copy-start.4
  3.6 0.7 %copy-done.4 = s32[32,5]{0,1:T(8,128)S(1)} copy-done((s32[32,5]{0,1:T(8,128)S(1)}, s32[32,5]{0,1:T(8,128)}, u32[]{:S(2)}) %copy-start.4) | copy-done | bytes 664
  4.3 0.0 copy-start.5
  4.3 0.7 %copy-done.5 = s32[1024]{0:T(1024)S(1)} copy-done((s32[1024]{0:T(1024)S(1)}, s32[1024]{0:T(1024)}, u32[]{:S(2)}) %copy-start.5) | copy-done | bytes 4120
  5.0 0.0 copy-start.6
  5.0 0.7 %copy-done.6 = s32[1024]{0:T(1024)S(1)} copy-done((s32[1024]{0:T(1024)S(1)}, s32[1024]{0:T(1024)}, u32[]{:S(2)}) %copy-start.6) | copy-done | bytes 4120
  5.7 51.8 %decode.1 = bf16[512,128]{1,0:T(8,128)(2,1)S(1)} custom-call(bf16[160,128,256]{2,1,0:T(8,128)(2,1)} %bitcast.30, bf16[1024,256]{1,0:T(8,128)(2,1)S(1)} %copy-done, bf16[32,16,128]{2,1,0:T(8,128)(2,1)S(1)} %bitcast.25, bf16[128,128]{1,0:T(8,128)(2,1)S(1)} %bitcast.27, bf16[32,4,128]{2,1,0:T(4,128)(2,1)S(1)} %bitcast.28, bf16[512,128]{1,0:T(8,128)(2,1)S(1)} %bitcast.26, ...), custom_call_target="tpu_custom_call" | custom-call | tf_op jit(solution)/shard_map/decode/pallas_call | solution.py:376
  57.4 0.7 %copy.14 = bf16[128,2,256]{2,1,0:T(2,128)(2,1)} copy(bf16[128,2,256]{2,1,0:T(2,128)(2,1)S(1)} %bitcast.24) | data formatting | bytes 262144
Async XLA Ops:
  0.0 1.0 %copy-start = (bf16[1024,256]{1,0:T(8,128)(2,1)S(1)}, bf16[1024,256]{1,0:T(8,128)(2,1)}, u32[]{:S(2)}) copy-start(bf16[1024,256]{1,0:T(8,128)(2,1)} %weight.1) | copy-start | bytes 1572868
  1.0 0.9 %copy-start.1 = (bf16[32,2,1024]{2,1,0:T(2,128)(2,1)S(1)}, bf16[32,2,1024]{2,1,0:T(2,128)(2,1)}, u32[]{:S(2)}) copy-start(bf16[32,2,1024]{2,1,0:T(2,128)(2,1)} %param.12) | copy-start | bytes 393220
  1.9 0.9 %copy-start.2 = (bf16[128,2,256]{2,1,0:T(2,128)(2,1)S(1)}, bf16[128,2,256]{2,1,0:T(2,128)(2,1)}, u32[]{:S(2)}) copy-start(bf16[128,2,256]{2,1,0:T(2,128)(2,1)} %param.15) | copy-start | bytes 393220
  2.9 0.8 %copy-start.3 = (bf16[32,2,1,256]{3,1,2,0:T(2,128)(2,1)S(1)}, bf16[32,2,1,256]{3,1,2,0:T(2,128)(2,1)}, u32[]{:S(2)}) copy-start(bf16[32,2,1,256]{3,1,2,0:T(2,128)(2,1)} %param.13) | copy-start | bytes 98308
  3.6 0.7 %copy-start.4 = (s32[32,5]{0,1:T(8,128)S(1)}, s32[32,5]{0,1:T(8,128)}, u32[]{:S(2)}) copy-start(s32[32,5]{0,1:T(8,128)} %param.9) | copy-start | bytes 1924
  4.3 0.7 %copy-start.5 = (s32[1024]{0:T(1024)S(1)}, s32[1024]{0:T(1024)}, u32[]{:S(2)}) copy-start(s32[1024]{0:T(1024)} %lengths.1) | copy-start | bytes 12292
  5.0 0.7 %copy-start.6 = (s32[1024]{0:T(1024)S(1)}, s32[1024]{0:T(1024)}, u32[]{:S(2)}) copy-start(s32[1024]{0:T(1024)} %new_slot.1) | copy-start | bytes 12292

commit v2 on v1

--- a/solution.py
+++ b/solution.py
@@ -43,7 +43,7 @@
     pool, weight, queries, fresh2, fresh3, residual, table, lengths, new_slot, out,
     pool_v, w_v, q_v, f2_v, f3_v, res_v, fv_v, att_v, attended, qx_s, qx_r, ret_s, ret_r,
     c_s, c_r, own_v, y_s, y_r, x_r, perm_v,
-    l_sem, qx_sem, ret_sem, w_ss, w_rs, z_ss, z_rs, c_ss, c_rs, y_ss, y_rs, x_ss, x_rs,
+    l_sem, qx_sem, ret_sem, w_ss, w_rs, z_ss, z_rs, c_ss, c_rs, y_ss, y_rs, x_ss, x_rs, ready,
 ):
     req, head = lax.axis_index("req"), lax.axis_index("head")
     x, core = head // 2, head % 2
@@ -63,12 +63,21 @@
         )
 
     barrier = pltpu.get_barrier_semaphore()
-    peers = [at(dz=d) for d in (1, 7, 2, 6)]
-    peers += [at(dy=d) for d in (1, 3, 2)]
-    peers += [at(dx=d) for d in (1, 3, 2)]
-    peers += [at(flip=1)]
-    for peer in peers:
+    for peer in [at(dy=d) for d in (1, 3, 2)] + [at(dx=d) for d in (1, 3, 2)] + [at(flip=1)]:
         pl.semaphore_signal(barrier, inc=1, device_id=peer, device_id_type=MESH)
+
+    def rank_of(place):
+        return place - (place // 4) * (place - 4)
+
+    rank = rank_of(z)
+    ahead = [rank - rank_of((z + d) % 8) for d in (1, 7, 2, 6)]
+    before = sum((a + 8) // 8 for a in ahead)
+    behind = 4 - before
+    for d, a in zip((1, 7, 2, 6), ahead):
+
+        @pl.when(a <= 0)
+        def _():
+            pl.semaphore_signal(barrier, inc=1, device_id=at(dz=d), device_id_type=MESH)
 
     load_q = pltpu.make_async_copy(queries, q_v, l_sem.at[0])
     load_f2 = pltpu.make_async_copy(fresh2, f2_v, l_sem.at[1])
@@ -97,7 +106,13 @@
         ).astype(jnp.bfloat16)
     fv_v[...] = pltpu.roll(f2_v[...].astype(jnp.float32), 126, 0).astype(jnp.bfloat16)
 
-    pl.semaphore_wait(barrier, len(peers))
+    pl.semaphore_wait(barrier, 7 + before)
+    for d, a in zip((1, 7, 2, 6), ahead):
+
+        @pl.when(a > 0)
+        def _():
+            pl.semaphore_signal(ready, inc=1, device_id=at(dz=d), device_id_type=MESH)
+
 
     send_q = remote(qx_s, qx_r, qx_sem.at[0], qx_sem.at[1], at(dy=2))
     send_q.start()
@@ -137,24 +152,35 @@
     lane = lax.broadcasted_iota(jnp.int32, (16, 128), 1)
     odd = (lax.broadcasted_iota(jnp.int32, (16, 128), 0) & 1) == 1
 
-    def attend(query, old, keys_new, values_new, place):
-        span = lengths[req * 32 + old]
-        pages = [table[p, old] for p in range(5)]
+    def attend(requests):
+        pages = [[table[p, r[1]] for p in range(5)] for r in requests]
         scores = []
-        for p in range(5):
-            s = dot(query, pool_v[pages[p], :, 0:128], NT) * scaling
-            scores.append(jnp.where(lane < span - 128 * p, s, NEG_FILL))
-        s = dot(query, keys_new, NT) * scaling
-        seen = (lane == place) | ((lane == place + 1) & odd)
-        scores.append(jnp.where(seen, s, NEG_FILL))
-        top = functools.reduce(jnp.maximum, scores)
-        top = jnp.max(top, axis=1, keepdims=True)
-        weights = [jnp.exp(s - top) for s in scores]
-        total = jnp.sum(functools.reduce(jnp.add, weights), axis=1, keepdims=True)
-        mixed = dot(weights[5].astype(jnp.bfloat16), values_new)
-        for p in range(5):
-            mixed += dot(weights[p].astype(jnp.bfloat16), pool_v[pages[p], :, 128:256])
-        return mixed / total
+        for (query, old, keys_new, _, place), own in zip(requests, pages):
+            span = lengths[req * 32 + old]
+            parts = []
+            for p in range(5):
+                s = dot(query, pool_v[own[p], :, 0:128], NT) * scaling
+                parts.append(jnp.where(lane < span - 128 * p, s, NEG_FILL))
+            s = dot(query, keys_new, NT) * scaling
+            seen = (lane == place) | ((lane == place + 1) & odd)
+            parts.append(jnp.where(seen, s, NEG_FILL))
+            scores.append(parts)
+        tops = [
+            jnp.max(functools.reduce(jnp.maximum, parts), axis=1, keepdims=True)
+            for parts in scores
+        ]
+        weights = [[jnp.exp(s - top) for s in parts] for parts, top in zip(scores, tops)]
+        totals = [
+            jnp.sum(functools.reduce(jnp.add, parts), axis=1, keepdims=True)
+            for parts in weights
+        ]
+        results = []
+        for (_, _, _, values_new, _), own, parts in zip(requests, pages, weights):
+            mixed = dot(parts[5].astype(jnp.bfloat16), values_new)
+            for p in range(5):
+                mixed += dot(parts[p].astype(jnp.bfloat16), pool_v[own[p], :, 128:256])
+            results.append(mixed)
+        return [mixed / total for mixed, total in zip(results, totals)]
 
     def slot_at(p):
         slot = jnp.where(p == low, jnp.where(high == 30, 31, 30), p)
@@ -163,13 +189,14 @@
         return jnp.where(p == 31, high, slot)
 
     def group(c):
+        requests = []
         for k in range(8):
             slot = slot_at(jnp.int32(c * 8 + k))
             v = new_slot[req * 32 + slot]
             old = jnp.where((v >> 5) == req, v & 31, slot)
-            att_v[k * 16 : k * 16 + 16] = attend(
-                q_v[slot], old, f2_v[...], fv_v[...], slot * 4
-            )
+            requests.append((q_v[slot], old, f2_v[...], fv_v[...], slot * 4))
+        for k, result in enumerate(attend(requests)):
+            att_v[k * 16 : k * 16 + 16] = result
 
     def chunk(c):
         return attended.at[z, pl.ds(c * 16, 16)]
@@ -184,49 +211,61 @@
                 jnp.concatenate(rows, 0).astype(jnp.bfloat16)
             )
         sends = [
-            remote(chunk(c), chunk(c), z_ss.at[c, k], z_rs.at[c, k], at(dz=dz))
+            remote(chunk(c), chunk(c), z_ss.at[c, k], z_rs.at[c, z], at(dz=dz))
             for k, dz in enumerate((1, 7, 2, 6))
         ]
         for k in (2, 3, 0, 1):
             sends[k].start()
         return sends
 
-    def arrive(dz, c, k):
-        remote(block(dz, c), block(dz, c), z_ss.at[c, k], z_rs.at[c, k], at(dz=1)).wait_recv()
+    def held(source, c):
+        return attended.at[source, pl.ds(c * 16, 16)]
+
+    def arrive(source, c):
+        remote(
+            held(source, c), held(source, c), z_ss.at[c, 0], z_rs.at[c, source], at(dz=1)
+        ).wait_recv()
+
+    def z_hop(source, c, n, dz):
+        return remote(
+            held(source, c), held(source, c), z_ss.at[c, n], z_rs.at[c, source], at(dz=dz)
+        )
 
     def forward(c):
-        sends = []
-        arrive(6, c, 2)
-        sends.append(remote(block(6, c), block(6, c), z_ss.at[c, 4], z_rs.at[c, 4], at(dz=1)))
-        if c % 2 == 0:
-            sends.append(
-                remote(block(6, c), block(6, c), z_ss.at[c, 6], z_rs.at[c, 6], at(dz=2))
-            )
-        for send in sends:
-            send.start()
-        arrive(2, c, 3)
-        more = [remote(block(2, c), block(2, c), z_ss.at[c, 5], z_rs.at[c, 5], at(dz=7))]
-        if c % 2 == 1:
-            more.append(
-                remote(block(2, c), block(2, c), z_ss.at[c, 6], z_rs.at[c, 6], at(dz=6))
-            )
-        for send in more:
-            send.start()
-        return sends + more
+        for here in range(8):
+
+            @pl.when(z == here)
+            def _():
+                for k, near, n, far, parity in ((6, 1, 4, 2, 0), (2, 7, 5, 6, 1)):
+                    source = (here + k) % 8
+                    arrive(source, c)
+                    z_hop(source, c, n, near).start()
+                    if c % 2 == parity:
+                        z_hop(source, c, 6, far).start()
+
+        return [z_hop(0, c, n, 1) for n in (4, 5, 6)]
 
     z_sends = []
     group(0)
+
+    @pl.when(behind > 0)
+    def _():
+        pl.semaphore_wait(ready, behind)
+
     z_sends += publish(0)
 
     send_q.wait_recv()
     pad = jnp.zeros((112, 128), jnp.bfloat16)
-    for k, old in enumerate((i0, i1)):
-        result = attend(
+    leaving = [
+        (
             qx_r[k, 0:16], old,
             jnp.concatenate([qx_r[k, 16:32], pad], 0),
             jnp.concatenate([qx_r[k, 32:48], pad], 0),
             0,
         )
+        for k, old in enumerate((i0, i1))
+    ]
+    for k, result in enumerate(attend(leaving)):
         ret_s[k] = result.astype(jnp.bfloat16)
     send_ret = remote(ret_s, ret_r, ret_sem.at[0], ret_sem.at[1], at(dy=2))
     send_ret.start()
@@ -254,52 +293,28 @@
             remote(w_half(d, half), w_half(2, half), w_ss.at[k], w_rs.at[k], at(dy=dy))
         )
         w_fwd[-1].start()
-    for c in (1, 2, 3):
-        z_sends += forward(c)
-    for c in range(4):
-        arrive(7, c, 0)
-        arrive(1, c, 1)
-        arrive(5, c, 4)
-        arrive(3, c, 5)
-        arrive(4, c, 6)
-
-    def rows_of(which):
-        return attended[pl.ds(which * 4, 4)].reshape(256, 1024)
-
-    def core_copy(d):
-        return remote(c_s.at[d], c_r.at[d], c_ss.at[d], c_rs.at[d], at(flip=1))
-
-    def y_copy(d):
-        return remote(y_s.at[d], y_r.at[d], y_ss.at[d], y_rs.at[d], at(dy=d))
-
-    def product(which, d):
-        return dot(rows_of(which), w_v[d])
-
-    def away(d):
-        c_s[d] = product(1 - core, d).astype(jnp.bfloat16)
-        core_copy(d).start()
-
-    def near(d):
-        own_v[d] = product(core, d)
-
-    def join(d):
-        core_copy(d).wait_recv()
-        both = own_v[d] + c_r[d].astype(jnp.float32)
-        both = both.astype(jnp.bfloat16).reshape(4, 64, 256)
-        if d == 0:
-            y_r[0] = both
-        else:
-            y_s[d] = both
-            y_copy(d).start()
-
-    def x_move(d):
+    def source_of(t):
+        return t if t < 4 else 11 - t
+
+    def core_copy(t):
+        n = t % 4
+        return remote(c_s.at[t], c_r.at[n], c_ss.at[n], c_rs.at[n], at(flip=1))
+
+    def y_copy(d, n):
+        return remote(
+            y_s.at[d, n], y_r.at[d, n], y_ss.at[d, n], y_rs.at[d, n], at(dy=d)
+        )
+
+    def x_move(d, n):
         i = (y + 4 - d) % 4
-        far = remote(y_r.at[d], x_r.at[:, x], x_ss.at[d], x_rs.at[x], (req, i * 2 + core))
-        here = pltpu.make_async_copy(y_r.at[d], x_r.at[:, x], x_ss.at[d])
+        far = remote(
+            y_r.at[d, n], x_r.at[n, x], x_ss.at[d, n], x_rs.at[x, n], (req, i * 2 + core)
+        )
+        here = pltpu.make_async_copy(y_r.at[d, n], x_r.at[n, x], x_ss.at[d, n])
         return i != x, far, here
 
-    def x_start(d):
-        other, far, here = x_move(d)
+    def x_start(d, n):
+        other, far, here = x_move(d, n)
 
         @pl.when(other)
         def _():
@@ -309,59 +324,114 @@
         def _():
             here.start()
 
+    def multiply(t):
+        source = source_of(t)
+        k = (source + 8 - z) % 8
+
+        @pl.when((k != 0) & (k != 2) & (k != 6))
+        def _():
+            for c in range(4):
+                arrive(source, c)
+
+        rows = attended[source]
+        for d in range(4):
+            part = dot(rows, w_v[d])
+            own_v[t, d] = part
+            c_s[t, d] = part.astype(jnp.bfloat16)
+
+        @pl.when(core != t // 4)
+        def _():
+            core_copy(t).start()
+
+    def join(t):
+        n = t % 4
+
+        @pl.when(core == t // 4)
+        def _():
+            core_copy(t).wait_recv()
+            for d in (2, 1, 3, 0):
+                both = (own_v[t, d] + c_r[n, d].astype(jnp.float32)).astype(jnp.bfloat16)
+                if d == 0:
+                    y_r[0, n] = both
+                    x_start(0, n)
+                else:
+                    y_s[d, n] = both
+                    y_copy(d, n).start()
+
+    def relay(t):
+        @pl.when(core == t // 4)
+        def _():
+            for d in (1, 3, 2):
+                y_copy(d, t % 4).wait_recv()
+                x_start(d, t % 4)
+
+    def finish(t):
+        n = t % 4
+        for k in range(4):
+
+            @pl.when(k != x)
+            def _():
+                remote(
+                    y_r.at[0, n], x_r.at[n, k], x_ss.at[0, n], x_rs.at[k, n], at(dx=1)
+                ).wait_recv()
+
+        for d in range(4):
+            other, far, here = x_move(d, n)
+
+            @pl.when(other)
+            def _():
+                far.wait_send()
+
+            @pl.when(jnp.logical_not(other))
+            def _():
+                here.wait()
+
+        q = source_of(t) - t // 4 * 4
+        parts = x_r[n].reshape(256, 256)
+        total = dot(perm_v[q, 0], parts[:, 0:128]) + dot(perm_v[q, 1], parts[:, 128:256])
+        rows = pl.ds(q * 128, 128)
+        total += res_v[rows].astype(jnp.float32)
+        out[rows] = total.astype(jnp.bfloat16)
+
+    z_sends += forward(1)
+    z_sends += forward(2)
+    z_sends += forward(3)
     w_own[2].wait_recv()
     w_own[3].wait_recv()
-    for d in (1, 3, 0):
-        away(d)
-    for d in (1, 3, 0):
-        near(d)
-    for d in (1, 3):
-        join(d)
-    for k in (4, 5):
-        w_fwd[k - 4].wait_recv()
-    away(2)
-    near(2)
-    join(0)
-    x_start(0)
-    join(2)
-    for d in (1, 3, 2):
-        y_copy(d).wait_recv()
-        x_start(d)
-
-    for d in range(4):
-        other, far, here = x_move(d)
-
-        @pl.when(other)
-        def _():
-            far.wait_send()
-
-        @pl.when(jnp.logical_not(other))
-        def _():
-            here.wait()
-
-    for k in range(4):
-
-        @pl.when(k != x)
-        def _():
-            remote(
-                y_r.at[0], x_r.at[:, k], x_ss.at[0], x_rs.at[k], at(dx=1)
-            ).wait_recv()
+    for fwd in w_fwd:
+        fwd.wait_recv()
+    for t in range(8):
+        multiply(t)
+        if t >= 1:
+            join(t - 1)
+        if t >= 4:
+            relay(t - 4)
+    join(7)
+    for t in range(4, 8):
+        relay(t)
 
     load_res.wait()
-    for q in range(4):
-        parts = x_r[q].reshape(256, 256)
-        total = dot(perm_v[q, 0], parts[:, 0:128]) + dot(perm_v[q, 1], parts[:, 128:256])
-        total += res_v[q * 128 : q * 128 + 128].astype(jnp.float32)
-        out[q * 128 : q * 128 + 128] = total.astype(jnp.bfloat16)
+    for first in (0, 4):
+
+        @pl.when(core == first // 4)
+        def _():
+            for t in range(first, first + 4):
+                finish(t)
 
     send_q.wait_send()
     send_ret.wait_send()
     for send in w_own + w_fwd + z_sends:
         send.wait_send()
-    for d in range(4):
-        core_copy(d).wait_send()
-    for d in (1, 2, 3):
-        y_copy(d).wait_send()
+    for t in range(8):
+
+        @pl.when(core != t // 4)
+        def _():
+            core_copy(t).wait_send()
+
+        @pl.when(core == t // 4)
+        def _():
+            for d in (1, 2, 3):
+                y_copy(d, t % 4).wait_send()
 
 
 def per_device(kv_pool, block_table, lengths, new_slot, queries, new_kv, output_weight, residual):
@@ -376,7 +446,7 @@
     out = pl.pallas_call(
         kernel,
         name="decode",
-        out_shape=jax.ShapeDtypeStruct((512, 128), bf16),
+        out_shape=pltpu.VMEM((512, 128), bf16),
         in_specs=[hbm] * 6 + [smem] * 3,
         out_specs=vmem,
         scratch_shapes=[
@@ -393,9 +463,9 @@
             pltpu.VMEM((2, 48, 128), bf16),
             pltpu.VMEM((2, 16, 128), bf16),
             pltpu.VMEM((2, 16, 128), bf16),
-            pltpu.VMEM((4, 256, 256), bf16),
-            pltpu.VMEM((4, 256, 256), bf16),
-            pltpu.VMEM((4, 256, 256), f32),
+            pltpu.VMEM((8, 4, 64, 256), bf16),
+            pltpu.VMEM((4, 4, 64, 256), bf16),
+            pltpu.VMEM((8, 4, 64, 256), f32),
             pltpu.VMEM((4, 4, 64, 256), bf16),
             pltpu.VMEM((4, 4, 64, 256), bf16),
             pltpu.VMEM((4, 4, 64, 256), bf16),
@@ -406,16 +476,17 @@
             sem((6,)),
             sem((6,)),
             sem((4, 7)),
-            sem((4, 7)),
+            sem((4, 8)),
             sem((4,)),
             sem((4,)),
-            sem((4,)),
-            sem((4,)),
-            sem((4,)),
-            sem((4,)),
+            sem((4, 4)),
+            sem((4, 4)),
+            sem((4, 4)),
+            sem((4, 4)),
+            pltpu.SemaphoreType.REGULAR,
         ],
         compiler_params=pltpu.CompilerParams(
-            collective_id=0, has_side_effects=True, vmem_limit_bytes=48 << 20
+            collective_id=0, has_side_effects=True, vmem_limit_bytes=60 << 20
         ),
     )(
         kv_pool.reshape(160, 128, 256), output_weight, q, fresh.reshape(128, 128),

time: 58.4 us -> 42.8 us (0.73)
  the two profiles are of different devices: /device:TPU:4 before, /device:TPU:9 now
where the time goes in v2:
time: 42.8 us; the launch traced here: 42.7 us
  Pallas kernels  42.1 us (98%)
  local copies, waits for them, and re-layouts  0.66 us (2%)
    pallas_call x1, Pallas kernels, per_device(): pl.pallas_call(kernel, name='decode', out_shape=pltpu.VMEM((512, 128), bf...  42.1 us

profile of v2, /device:TPU:9, one launch (start us, length us, event | category | flops | bytes accessed | tf_op | source)
XLA Modules:
  0.0 42.7 jit_solution(3749807257430241717)
XLA Ops:
  0.0 42.1 %decode.1 = bf16[512,128]{1,0:T(8,128)(2,1)S(1)} custom-call(bf16[160,128,256]{2,1,0:T(8,128)(2,1)} %bitcast.25, bf16[1024,256]{1,0:T(8,128)(2,1)} %weight.1, bf16[32,16,128]{2,1,0:T(8,128)(2,1)} %bitcast.26, bf16[128,128]{1,0:T(8,128)(2,1)} %bitcast.28, bf16[32,4,128]{2,1,0:T(4,128)(2,1)} %bitcast.29, bf16[512,128]{1,0:T(8,128)(2,1)} %bitcast.27, ...), custom_call_target="tpu_custom_call" | custom-call | tf_op jit(solution)/shard_map/decode/pallas_call | solution.py:446
  42.1 0.7 %copy.14 = bf16[128,2,256]{2,1,0:T(2,128)(2,1)} copy(bf16[128,2,256]{2,1,0:T(2,128)(2,1)S(1)} %bitcast.24) | data formatting | bytes 262144

commit v3 on v2

--- a/solution.py
+++ b/solution.py
@@ -253,6 +253,8 @@
         pl.semaphore_wait(ready, behind)
 
     z_sends += publish(0)
+    group(1)
+    z_sends += publish(1)
 
     send_q.wait_recv()
     pad = jnp.zeros((112, 128), jnp.bfloat16)
@@ -272,8 +274,6 @@
     w_own[2].start()
     w_own[3].start()
 
-    group(1)
-    z_sends += publish(1)
     group(2)
     z_sends += publish(2)
     group(3)
@@ -404,10 +404,8 @@
         multiply(t)
         if t >= 1:
             join(t - 1)
-        if t >= 4:
-            relay(t - 4)
     join(7)
-    for t in range(4, 8):
+    for t in range(8):
         relay(t)
 
     load_res.wait()

time: 42.8 us -> 42.5 us (level); the launches traced: 42.7 us -> 41.6 us
  Pallas kernels: 42.1 us -> 41 us
    pallas_call x1, Pallas kernels: 42.1 us -> 41 us  [per_device(): pl.pallas_call(kernel, name='decode', out_shape=pltpu.VMEM((512, 128), bf...]
where the time goes in v3:
time: 42.5 us; the launch traced here: 41.6 us
  Pallas kernels  41 us (96%)
  local copies, waits for them, and re-layouts  0.66 us (2%)
    pallas_call x1, Pallas kernels, per_device(): pl.pallas_call(kernel, name='decode', out_shape=pltpu.VMEM((512, 128), bf...  41 us

profile of v3, /device:TPU:9, one launch (start us, length us, event | category | flops | bytes accessed | tf_op | source)
XLA Modules:
  0.0 41.6 jit_solution(11703214952717049378)
XLA Ops:
  0.0 41.0 %decode.1 = bf16[512,128]{1,0:T(8,128)(2,1)S(1)} custom-call(bf16[160,128,256]{2,1,0:T(8,128)(2,1)} %bitcast.25, bf16[1024,256]{1,0:T(8,128)(2,1)} %weight.1, bf16[32,16,128]{2,1,0:T(8,128)(2,1)} %bitcast.26, bf16[128,128]{1,0:T(8,128)(2,1)} %bitcast.28, bf16[32,4,128]{2,1,0:T(4,128)(2,1)} %bitcast.29, bf16[512,128]{1,0:T(8,128)(2,1)} %bitcast.27, ...), custom_call_target="tpu_custom_call" | custom-call | tf_op jit(solution)/shard_map/decode/pallas_call | solution.py:444
  41.0 0.7 %copy.14 = bf16[128,2,256]{2,1,0:T(2,128)(2,1)} copy(bf16[128,2,256]{2,1,0:T(2,128)(2,1)S(1)} %bitcast.24) | data formatting | bytes 262144
